TPU v7x, 32 devices: a whole 2x2x4 slice. The times are simulated.
32 devices in a mesh: feat: 8 (over y, x, core), grp: 4 (over z).
Axes of the slice: x: 2, y: 2, z: 4, core: 2. Of those that a mesh axis runs over, the one named last changes fastest.
Arguments:
- node_features: bfloat16 [2048, 32768], P('feat', 'grp'), may hold values from -6 to 6
- neighbours: int32 [64, 16, 512], P('grp'), may hold values from 0 to 511, as said below
- edge_counts: int32 [64, 512], P('grp'), may hold values from 0 to 16, as said below
- first_weight_matrix: bfloat16 [2048, 2048], P(('feat', 'grp')), may hold values from -0.25 to 0.25
- bias_one: bfloat16 [2048], P(('feat', 'grp')), may hold values from -3 to 3
- weight_two: bfloat16 [2048, 2048], P(('feat', 'grp')), may hold values from -0.25 to 0.25
- bias_two: bfloat16 [2048], P(('feat', 'grp')), may hold values from -3 to 3
- cotangent: bfloat16 [2048, 32768], P(None, ('grp', 'feat')), may hold values from -6 to 6
Outputs:
- layer_output: bfloat16 [2048, 32768], P(None, ('grp', 'feat'))
- input_grad: float32 [2048, 32768], P('feat', 'grp')
- grad_weight_one: float32 [2048, 2048], P(('feat', 'grp'))
- grad_bias_one: float32 [2048], P(('feat', 'grp'))
- grad_weight_two: float32 [2048, 2048], P(('feat', 'grp'))
- grad_bias_two: float32 [2048], P(('feat', 'grp'))
Inputs may be any that keep to these rules, and one draw needn't show every extreme that they name: `edge_counts`: in each cluster the nodes with edges are a prefix of its 512 slots, at least half of them, and one cluster of every draw uses all slots; such a node has 1 to 16 edges, one node of each cluster exactly 16; slots after the prefix have 0. `neighbours`: every entry names a slot inside its cluster's prefix of nodes with edges; entries at k >= edge_counts are not edges.
All inputs are finite; a program needn't handle non-finite values.
Results may differ from a plain program's by a relative error of at most 0.01.
Values may be sent and summed in bfloat16 or wider, within the bound.
A program may use at most 256 MiB of HBM per device.

v0:
```python
import jax
import jax.numpy as jnp
from jax import lax
from jax.sharding import PartitionSpec as P


def activate(value):
    return jax.nn.gelu(value, approximate=True)


def count_matrix(neighbours, edge_counts):
    capacity = neighbours.shape[2]
    positions = jnp.arange(capacity, dtype=jnp.int32)
    columns = jnp.arange(neighbours.shape[1], dtype=jnp.int32)

    def cluster_block(cluster_item):
        targets, totals = cluster_item
        usable = columns[:, None] < totals[None, :]
        equality_mask = (targets[:, :, None] == positions[None, None, :]) & usable[:, :, None]
        return jnp.sum(equality_mask.astype(jnp.float32), axis=0).astype(jnp.bfloat16)

    return lax.map(cluster_block, (neighbours, edge_counts))


def to_rows(field):
    return lax.all_to_all(field, "feat", split_axis=1, concat_axis=0, tiled=True)


def grad_to_features(field):
    return lax.all_to_all(field, "feat", split_axis=0, concat_axis=1, tiled=True)


def linear_grads(rows, grad_pre, weight):
    weight_term = lax.dot_general(
        rows, grad_pre, (((1,), (1,)), ((), ())), preferred_element_type=jnp.float32
    )
    bias_term = jnp.sum(grad_pre.astype(jnp.float32), axis=1)
    grad_rows = jnp.dot(weight, grad_pre, preferred_element_type=jnp.float32)
    return (weight_term, bias_term, grad_rows.astype(jnp.bfloat16))


def apply_linear(rows, weight, bias):
    product = lax.dot_general(
        weight, rows, (((0,), (0,)), ((), ())), preferred_element_type=jnp.float32
    )
    return product + bias.astype(jnp.float32)[:, None]


def body(
    node_features,
    neighbours,
    edge_counts,
    first_weight_matrix,
    bias_one,
    weight_two,
    bias_two,
    cotangent,
):
    clusters, capacity = edge_counts.shape
    tile_operator = count_matrix(neighbours, edge_counts)
    totals = edge_counts.astype(jnp.float32)
    scaling = jnp.where(edge_counts > 0, 1.0 / (totals + 1.0), jnp.zeros_like(totals))
    w_one, w_two, b_one, b_two = (
        lax.all_gather(first_weight_matrix, ("feat", "grp"), axis=0, tiled=True),
        lax.all_gather(weight_two, ("feat", "grp"), axis=0, tiled=True),
        lax.all_gather(bias_one, ("feat", "grp"), axis=0, tiled=True),
        lax.all_gather(bias_two, ("feat", "grp"), axis=0, tiled=True),
    )

    def aggregate(field):
        cluster_blocks_padded = field.reshape(field.shape[0], clusters, capacity)
        summed_rows = jnp.einsum(
            "sma,usa->usm", tile_operator, cluster_blocks_padded, preferred_element_type=jnp.float32
        )
        summed_rows = summed_rows + 2.0 * cluster_blocks_padded.astype(jnp.float32)
        return (scaling[None, :, :] * summed_rows).reshape(field.shape[0], field.shape[1])

    def distribute_reverse(grad):
        cluster_blocks_padded = grad.reshape(grad.shape[0], clusters, capacity).astype(jnp.float32)
        normed_lines = (scaling[None, :, :] * cluster_blocks_padded).astype(jnp.bfloat16)
        summed_rows = jnp.einsum(
            "xcv,nxc->nxv", tile_operator, normed_lines, preferred_element_type=jnp.float32
        )
        summed_rows = summed_rows + 2.0 * normed_lines.astype(jnp.float32)
        return summed_rows.reshape(grad.shape[0], grad.shape[1])

    def forward_pass(features, initial_linear_kernel, first_b, second_w, second_b):
        rows_one = to_rows(aggregate(features).astype(jnp.bfloat16))
        pre_one = apply_linear(rows_one, initial_linear_kernel, first_b)
        hidden_rows = activate(pre_one).astype(jnp.bfloat16)
        hidden = lax.all_to_all(hidden_rows, "feat", split_axis=0, concat_axis=1, tiled=True)
        rows_two = to_rows(aggregate(hidden).astype(jnp.bfloat16))
        pre_two = apply_linear(rows_two, second_w, second_b)
        return (rows_one, pre_one, rows_two, pre_two)

    kept = forward_pass(node_features, w_one, b_one, w_two, b_two)
    layer_output = activate(kept[3]).astype(jnp.bfloat16)
    fresh = lax.optimization_barrier((node_features, w_one, b_one, w_two, b_two))
    rows_one, pre_one, rows_two, pre_two = forward_pass(
        fresh[0], fresh[1], fresh[2], fresh[3], fresh[4]
    )
    pullback_two = jax.vjp(activate, pre_two)[1]
    gradient_preact_second = pullback_two(cotangent.astype(jnp.float32))[0].astype(jnp.bfloat16)
    term_w_two, term_b_two, grad_rows_two = linear_grads(rows_two, gradient_preact_second, w_two)
    grad_hidden = distribute_reverse(grad_to_features(grad_rows_two)).astype(jnp.bfloat16)
    grad_hidden_rows = lax.all_to_all(grad_hidden, "feat", split_axis=1, concat_axis=0, tiled=True)
    first_layer_pullback = jax.vjp(activate, pre_one)[1]
    grad_pre_one = first_layer_pullback(grad_hidden_rows.astype(jnp.float32))[0].astype(
        jnp.bfloat16
    )
    term_w_one, term_b_one, grad_rows_one = linear_grads(rows_one, grad_pre_one, w_one)
    input_grad = distribute_reverse(grad_to_features(grad_rows_one))
    grad_w_one, grad_w_two, grad_b_one, grad_b_two = (
        lax.psum_scatter(term_w_one, ("feat", "grp"), scatter_dimension=0, tiled=True),
        lax.psum_scatter(term_w_two, ("feat", "grp"), scatter_dimension=0, tiled=True),
        lax.psum_scatter(term_b_one, ("feat", "grp"), scatter_dimension=0, tiled=True),
        lax.psum_scatter(term_b_two, ("feat", "grp"), scatter_dimension=0, tiled=True),
    )
    return (layer_output, input_grad, grad_w_one, grad_b_one, grad_w_two, grad_b_two)


def solution(mesh):
    in_specs = (
        P("feat", "grp"),
        P("grp", None, None),
        P("grp", None),
        P(("feat", "grp"), None),
        P(("feat", "grp")),
        P(("feat", "grp"), None),
        P(("feat", "grp")),
        P(None, ("grp", "feat")),
    )
    out_specs = (
        P(None, ("grp", "feat")),
        P("feat", "grp"),
        P(("feat", "grp"), None),
        P(("feat", "grp")),
        P(("feat", "grp"), None),
        P(("feat", "grp")),
    )
    return jax.shard_map(body, mesh=mesh, in_specs=in_specs, out_specs=out_specs, check_vma=False)
```

profile of v0, /device:TPU:0, one launch (start us, length us, event | category | flops | bytes accessed | tf_op | source)
XLA Modules:
  0.0 1149.6 jit_solution(7159046562380207922)
XLA Ops:
  11.2 43.2 %all-reduce.5 = (bf16[2048]{0:T(1024)(128)(2,1)S(1)}, bf16[2048]{0:T(1024)(128)(2,1)S(1)}) all-reduce(bf16[2048]{0:T(1024)(128)(2,1)S(1)} %dynamic-update-slice.1, bf16[2048]{0:T(1024)(128)(2,1)S(1)} %dynamic-update-slice), channel_id=1, replica_groups=mesh['feat'=8,'grp'=4] {'feat','grp'}, use_global_device_ids=true, to_apply=%add.1 | all-reduce | flops 4096 | bytes 16384
  54.5 94.7 %while.11 = (s32[]{:T(128)}, bf16[16,512,512]{2,1,0:T(8,128)(2,1)}, s32[16,16,512]{2,1,0:T(8,128)}, s32[16,512]{1,0:T(8,128)}, s32[]{:T(128)}) while((s32[]{:T(128)}, bf16[16,512,512]{2,1,0:T(8,128)(2,1)}, s32[16,16,512]{2,1,0:T(8,128)}, s32[16,512]{1,0:T(8,128)}, s32[]{:T(128)}) %tuple.34), condition=%wide.region_2.3_spmd.clone, body=%wide.region_0.2_spmd.clone.sunk | while | flops 16523266 | bytes 1693777 | solution.py:22
  56.0 3.6 convert_reduce_fusion.4
  61.9 3.6 convert_reduce_fusion.4
  67.8 3.6 convert_reduce_fusion.4
  132.9 3.6 convert_reduce_fusion.4
  149.1 21.1 %all-gather.5.cloned.1.call-done = bf16[2048,2048]{1,0:T(8,128)(2,1)} async-done(((bf16[64,2048]{1,0:T(8,128)(2,1)}), bf16[2048,2048]{1,0:T(8,128)(2,1)}) %all-gather.5.cloned.1.call-update) | async-done | bytes 8388624 | tf_op jit(solution)/shard_map/all_gather | solution.py:65
  170.3 6.4 copy.96
  176.6 8.6 fusion.42
  185.3 6.4 copy.99
  191.7 4.6 all-to-all-start.3
  196.3 49.1 %all-to-all-done.3 = bf16[256,8,1024]{2,0,1:T(8,128)(2,1)} async-done(((bf16[256,8,1024]{2,0,1:T(8,128)(2,1)}), bf16[256,8,1024]{2,0,1:T(8,128)(2,1)}, u32[]{:S(2)}, u32[]{:S(2)}) %all-to-all-start.3) | async-done | bytes 4194336 | tf_op jit(solution)/shard_map/all_to_all | solution.py:26
  245.4 16.9 %multiply_convert_fusion.2 = (bf16[2048,1024]{0,1:T(8,128)(2,1)S(1)}, f32[2048,1024]{0,1:T(8,128)}) fusion(f32[2048]{0:T(1024)S(1)} %convert_element_type.168, bf16[2048,2048]{1,0:T(8,128)(2,1)} %all-gather.3.cloned.1.call-done, bf16[2048,1024]{1,0:T(8,128)(2,1)} %bitcast.18), kind=kOutput, calls=%fused_computation.70 | convolution fusion | flops 8610906112 | bytes 25174016 | tf_op jit(solution)/shard_map/dot_general | solution.py:43
  262.6 51.9 %all_to_all.132 = bf16[8,256,1024]{1,2,0:T(8,128)(2,1)S(1)} all-to-all(bf16[8,256,1024]{1,2,0:T(8,128)(2,1)S(1)} %bitcast.135), channel_id=1, replica_groups=mesh['feat'=8,'grp'=4] {'feat'}, dimensions={0} | all-to-all | bytes 8388608 | tf_op jit(solution)/shard_map/all_to_all | solution.py:91
  314.5 3.9 fusion.40
  318.4 6.4 copy.104
  324.9 4.8 all-to-all-start.5
  329.7 6.4 copy.95
  336.2 42.6 %all-to-all-done.5 = bf16[256,8,1024]{2,0,1:T(8,128)(2,1)} async-done(((bf16[256,8,1024]{2,0,1:T(8,128)(2,1)}), bf16[256,8,1024]{2,0,1:T(8,128)(2,1)}, u32[]{:S(2)}, u32[]{:S(2)}) %all-to-all-start.5) | async-done | bytes 4194336 | tf_op jit(solution)/shard_map/all_to_all | solution.py:26
  378.8 20.0 %convert_reduce_fusion.1 = (f32[2048]{0:T(1024)}, bf16[2048,1024]{0,1:T(8,128)(2,1)S(1)}) fusion(f32[2048]{0:T(1024)S(1)} %convert_element_type.173, bf16[2048,2048]{1,0:T(8,128)(2,1)} %all-gather.5.cloned.1.call-done, bf16[2048,1024]{1,0:T(8,128)(2,1)} %bitcast.25, bf16[2048,1024]{0,1:T(8,128)(2,1)} %copy.95), kind=kOutput, calls=%fused_computation.66 | convolution fusion | flops 8640264192 | bytes 20987904 | tf_op jit(solution)/shard_map/dot_general | solution.py:43
  400.8 13.9 %fusion.49 = f32[2048,2048]{1,0:T(8,128)} fusion(bf16[2048,1024]{1,0:T(8,128)(2,1)} %bitcast.25, bf16[2048,1024]{0,1:T(8,128)(2,1)S(1)} %get-tuple-element.101), kind=kOutput, calls=%fused_computation.79 | convolution fusion | flops 8589934592 | bytes 25165824 | tf_op jit(solution)/shard_map/dot_general | solution.py:34
  415.2 12.6 %convolution_convert_fusion.1 = bf16[1024,2048]{1,0:T(8,128)(2,1)S(1)} fusion(bf16[2048,1024]{0,1:T(8,128)(2,1)} %copy-done.6, bf16[2048,2048]{1,0:T(8,128)(2,1)} %all-gather.5.cloned.1.call-done), kind=kOutput, calls=%fused_computation.76 | convolution fusion | flops 8592031744 | bytes 16777216 | tf_op jit(solution)/shard_map/dot_general | solution.py:38
  428.1 66.3 %all_to_all.133 = bf16[8,256,1024]{1,2,0:T(8,128)(2,1)S(1)} all-to-all(bf16[8,256,1024]{1,2,0:T(8,128)(2,1)S(1)} %bitcast.136), channel_id=1, replica_groups=mesh['feat'=8,'grp'=4] {'feat'}, dimensions={0} | all-to-all | bytes 8388608 | tf_op jit(solution)/shard_map/all_to_all | solution.py:30
  494.4 4.0 convert_element_type.200
  498.4 13.3 %fusion.38 = bf16[256,16,512]{0,2,1:T(8,128)(2,1)S(1)} fusion(bf16[16,512,512]{2,1,0:T(8,128)(2,1)} %get-tuple-element.43, f32[256,16,512]{0,2,1:T(8,128)} %bitcast.129, f32[16,512]{1,0:T(8,128)S(1)} %divide_select_fusion), kind=kOutput, calls=%fused_computation.52 | convolution fusion | flops 2164260864 | bytes 21004288 | tf_op jit(solution)/shard_map/xcv,nxc->nxv/dot_general | solution.py:81
  511.7 66.4 %all_to_all.134 = bf16[256,8,1024]{0,2,1:T(8,128)(2,1)S(1)} all-to-all(bf16[256,8,1024]{0,2,1:T(8,128)(2,1)S(1)} %bitcast.133), channel_id=1, replica_groups=mesh['feat'=8,'grp'=4] {'feat'}, dimensions={1} | all-to-all | bytes 8388608 | tf_op jit(solution)/shard_map/all_to_all | solution.py:106
  580.1 8.1 convert_reduce_fusion.2
  590.3 13.9 %fusion.48 = f32[2048,2048]{1,0:T(8,128)} fusion(bf16[2048,1024]{1,0:T(8,128)(2,1)} %bitcast.18, bf16[2048,1024]{0,1:T(8,128)(2,1)S(1)} %get-tuple-element.97), kind=kOutput, calls=%fused_computation.78 | convolution fusion | flops 8589934592 | bytes 25165824 | tf_op jit(solution)/shard_map/dot_general | solution.py:34
  604.2 6.4 copy.88
  610.6 8.8 fusion.46
  619.4 6.4 copy.90
  625.8 4.8 all-to-all-start
  630.6 63.8 %all-to-all-done = bf16[256,8,1024]{2,0,1:T(8,128)(2,1)} async-done(((bf16[256,8,1024]{2,0,1:T(8,128)(2,1)}), bf16[256,8,1024]{2,0,1:T(8,128)(2,1)}, u32[]{:S(2)}, u32[]{:S(2)}) %all-to-all-start) | async-done | bytes 4194336 | tf_op jit(solution)/shard_map/all_to_all | solution.py:26
  694.4 15.0 %fusion.29 = bf16[2048,1024]{0,1:T(8,128)(2,1)S(1)} fusion(f32[2048]{0:T(1024)S(1)} %convert_element_type.157, bf16[2048,1024]{1,0:T(8,128)(2,1)} %bitcast.4, bf16[2048,2048]{1,0:T(8,128)(2,1)} %all-gather.3.cloned.1.call-done), kind=kOutput, calls=%fused_computation.41 | convolution fusion | flops 8610906112 | bytes 16785408 | tf_op jit(solution)/shard_map/dot_general | solution.py:43
  709.7 66.7 %all_to_all.135 = bf16[8,256,1024]{1,2,0:T(8,128)(2,1)S(1)} all-to-all(bf16[8,256,1024]{1,2,0:T(8,128)(2,1)S(1)} %bitcast.137), channel_id=1, replica_groups=mesh['feat'=8,'grp'=4] {'feat'}, dimensions={0} | all-to-all | bytes 8388608 | tf_op jit(solution)/shard_map/all_to_all | solution.py:91
  776.4 3.9 fusion.44
  780.3 6.5 copy.94
  786.8 4.5 all-to-all-start.2
  791.3 12.6 %convolution_convert_fusion = bf16[1024,2048]{1,0:T(8,128)(2,1)S(1)} fusion(bf16[2048,1024]{0,1:T(8,128)(2,1)} %copy-done, bf16[2048,2048]{1,0:T(8,128)(2,1)} %all-gather.3.cloned.1.call-done), kind=kOutput, calls=%fused_computation.75 | convolution fusion | flops 8592031744 | bytes 16777216 | tf_op jit(solution)/shard_map/dot_general | solution.py:38
  806.2 48.9 %all-to-all-done.2 = bf16[256,8,1024]{2,0,1:T(8,128)(2,1)} async-done(((bf16[256,8,1024]{2,0,1:T(8,128)(2,1)}), bf16[256,8,1024]{2,0,1:T(8,128)(2,1)}, u32[]{:S(2)}, u32[]{:S(2)}) %all-to-all-start.2) | async-done | bytes 4194336 | tf_op jit(solution)/shard_map/all_to_all | solution.py:26
  855.1 4.8 all-to-all-start.8
  859.9 16.4 %fusion.37 = bf16[2048,1024]{0,1:T(8,128)(2,1)} fusion(f32[2048]{0:T(1024)S(1)} %convert_element_type.162, bf16[2048,1024]{1,0:T(8,128)(2,1)} %bitcast.12, bf16[2048,2048]{1,0:T(8,128)(2,1)} %all-gather.5.cloned.1.call-done), kind=kOutput, calls=%fused_computation.49 | convolution fusion | flops 8610906112 | bytes 16785408 | tf_op jit(solution)/shard_map/dot_general | solution.py:43
  876.3 6.4 copy.112
  882.7 77.0 %all-reduce.4 = (f32[2048]{0:T(1024)S(1)}, f32[2048]{0:T(1024)S(1)}) all-reduce(f32[2048]{0:T(1024)S(1)} %get-tuple-element.96, f32[2048]{0:T(1024)S(1)} %copy-done.5), channel_id=3, replica_groups=mesh['feat'=8,'grp'=4] {'feat','grp'}, use_global_device_ids=true, to_apply=%region_5.6.clone | all-reduce | flops 4096 | bytes 32768
  960.9 6.2 convert_element_type.202
  967.1 15.2 %bitcast_add_fusion = f32[256,16,512]{0,2,1:T(8,128)} fusion(bf16[16,512,512]{2,1,0:T(8,128)(2,1)} %get-tuple-element.43, f32[256,16,512]{0,2,1:T(8,128)} %bitcast.131, f32[16,512]{1,0:T(8,128)S(1)} %divide_select_fusion), kind=kOutput, calls=%fused_computation.50 | convolution fusion | flops 2162163712 | bytes 25198592 | tf_op jit(solution)/shard_map/xcv,nxc->nxv/dot_general | solution.py:81
  982.3 8.9 copy.113
  991.2 151.4 %reduce-scatter.3.cloned.1.call-done = f32[64,2048]{1,0:T(8,128)} async-done(((f32[2048,2048]{1,0:T(8,128)}), f32[64,2048]{1,0:T(8,128)}) %reduce-scatter.3.cloned.1.call-update) | async-done | bytes 524304 | tf_op jit(solution)/shard_map/reduce_scatter | solution.py:114
  (129 shorter events, 95.0 us)
Async XLA Ops:
  7.2 142.0 %all-gather.3.cloned.1.call-start = ((), (), s32[]{:S(2)}) async-start(), calls=%async_computation.11 | async-start | bytes 8650752 | tf_op jit(solution)/shard_map/all_gather | solution.py:64
  7.9 162.4 %all-gather.5.cloned.1.call-start = ((), (), s32[]{:S(2)}) async-start(), calls=%async_computation.12 | async-start | bytes 8650752 | tf_op jit(solution)/shard_map/all_gather | solution.py:65
  54.4 141.8 %copy-start.3 = (bf16[2048]{0:T(1024)(128)(2,1)}, bf16[2048]{0:T(1024)(128)(2,1)S(1)}, u32[]{:S(2)}) copy-start(bf16[2048]{0:T(1024)(128)(2,1)S(1)} %get-tuple-element.47) | copy-start | bytes 12292
  54.5 281.7 %copy-start.1 = (bf16[2048]{0:T(1024)(128)(2,1)}, bf16[2048]{0:T(1024)(128)(2,1)S(1)}, u32[]{:S(2)}) copy-start(bf16[2048]{0:T(1024)(128)(2,1)S(1)} %get-tuple-element.48) | copy-start | bytes 12292
  191.7 53.7 %all-to-all-start.3 = ((bf16[256,8,1024]{2,0,1:T(8,128)(2,1)}), bf16[256,8,1024]{2,0,1:T(8,128)(2,1)}, u32[]{:S(2)}, u32[]{:S(2)}) async-start(bf16[256,8,1024]{2,0,1:T(8,128)(2,1)} %copy.99), calls=%async_computation.3 | async-start | bytes 8388608 | tf_op jit(solution)/shard_map/all_to_all | solution.py:26
  262.3 52.2 %slice-start = ((s8[8388608]{0:T(1024)(128)(4,1)}), s8[4194304]{0:T(1024)(128)(4,1)S(1)}, s32[]{:S(2)}) async-start(s8[8388608]{0:T(1024)(128)(4,1)} %bitcast.125), calls=%async_computation.15 | async-start | bytes 8388608
  262.6 52.0 %slice-start.1 = ((s8[8388608]{0:T(1024)(128)(4,1)}), s8[4194304]{0:T(1024)(128)(4,1)S(1)}, s32[]{:S(2)}) async-start(s8[8388608]{0:T(1024)(128)(4,1)} %bitcast.125), calls=%async_computation.16 | async-start | bytes 8388608
  324.9 53.9 %all-to-all-start.5 = ((bf16[256,8,1024]{2,0,1:T(8,128)(2,1)}), bf16[256,8,1024]{2,0,1:T(8,128)(2,1)}, u32[]{:S(2)}, u32[]{:S(2)}) async-start(bf16[256,8,1024]{2,0,1:T(8,128)(2,1)} %copy.104), calls=%async_computation.5 | async-start | bytes 8388608 | tf_op jit(solution)/shard_map/all_to_all | solution.py:26
  329.7 661.6 %reduce-scatter.5.cloned.1.call-start = ((), (), s32[]{:S(2)}) async-start(), calls=%async_computation.14 | async-start | bytes 17301504 | tf_op jit(solution)/shard_map/reduce_scatter | solution.py:115
  398.8 2.0 copy-start.6
  414.7 727.9 %reduce-scatter.3.cloned.1.call-start = ((), (), s32[]{:S(2)}) async-start(), calls=%async_computation.13 | async-start | bytes 17301504 | tf_op jit(solution)/shard_map/reduce_scatter | solution.py:114
  588.3 2.0 copy-start
  619.4 11.2 copy-start.4
  625.8 68.6 %all-to-all-start = ((bf16[256,8,1024]{2,0,1:T(8,128)(2,1)}), bf16[256,8,1024]{2,0,1:T(8,128)(2,1)}, u32[]{:S(2)}, u32[]{:S(2)}) async-start(bf16[256,8,1024]{2,0,1:T(8,128)(2,1)} %copy.90), calls=%async_computation | async-start | bytes 8388608 | tf_op jit(solution)/shard_map/all_to_all | solution.py:26
  709.4 67.0 %slice-start.2 = ((s8[8388608]{0:T(1024)(128)(4,1)}), s8[4194304]{0:T(1024)(128)(4,1)S(1)}, s32[]{:S(2)}) async-start(s8[8388608]{0:T(1024)(128)(4,1)} %bitcast.127), calls=%async_computation.17 | async-start | bytes 8388608
  709.7 66.7 %slice-start.3 = ((s8[8388608]{0:T(1024)(128)(4,1)}), s8[4194304]{0:T(1024)(128)(4,1)S(1)}, s32[]{:S(2)}) async-start(s8[8388608]{0:T(1024)(128)(4,1)} %bitcast.127), calls=%async_computation.18 | async-start | bytes 8388608
  786.8 68.3 %all-to-all-start.2 = ((bf16[256,8,1024]{2,0,1:T(8,128)(2,1)}), bf16[256,8,1024]{2,0,1:T(8,128)(2,1)}, u32[]{:S(2)}, u32[]{:S(2)}) async-start(bf16[256,8,1024]{2,0,1:T(8,128)(2,1)} %copy.94), calls=%async_computation.2 | async-start | bytes 8388608 | tf_op jit(solution)/shard_map/all_to_all | solution.py:26
  803.9 56.0 %copy-start.2 = (bf16[2048]{0:T(1024)(128)(2,1)S(1)}, bf16[2048]{0:T(1024)(128)(2,1)}, u32[]{:S(2)}) copy-start(bf16[2048]{0:T(1024)(128)(2,1)} %copy-done.1) | copy-start | bytes 12292
  855.1 105.8 %all-to-all-start.8 = ((bf16[8,256,1024]{1,2,0:T(8,128)(2,1)}), bf16[8,256,1024]{1,2,0:T(8,128)(2,1)}, u32[]{:S(2)}, u32[]{:S(2)}) async-start(bf16[8,256,1024]{1,2,0:T(8,128)(2,1)} %bitcast.134), calls=%async_computation.8 | async-start | bytes 8388608 | tf_op jit(solution)/shard_map/all_to_all | solution.py:30
  876.3 6.4 copy-start.5
Sparse Core Ops, SparseCore 0:
  10.9 80.2 all-gather.2
  94.2 76.0 all-gather.4
  414.8 361.8 reduce-scatter.4
  779.5 363.1 reduce-scatter.2
where the time goes:
time: 1160 us; the launch traced here: 1150 us
  waiting for transfers between devices  378 us (33%)
  blocking collectives  372 us (32%)
  matrix products  175 us (15%)
  local copies, waits for them, and re-layouts  109 us (9%)
  other arithmetic  77.3 us (7%)
  starting transfers between devices  24 us (2%)
  between operations  14.5 us (1%)
    all_to_all x4, waiting for transfers between devices, to_rows(): lax.all_to_all(field, 'feat', split_axis=1, concat_axis=0, tiled=True)  204 us
    reduce_scatter x1, waiting for transfers between devices, body(): lax.psum_scatter(term_w_one, ('feat', 'grp'), scatter_dimension=0, tiled=...  151 us
    unnamed x2, blocking collectives  120 us
    all_to_all x2, blocking collectives, forward_pass(): lax.all_to_all(hidden_rows, 'feat', split_axis=0, concat_axis=1, tiled=True)  119 us
    dot_general x4, matrix products, apply_linear(): lax.dot_general(weight, rows, (((0,), (0,)), ((), ())), preferred_element...  68.3 us
    all_to_all x1, blocking collectives, body(): lax.all_to_all(grad_hidden, 'feat', split_axis=1, concat_axis=0, tiled=True)  66.4 us
    all_to_all x1, blocking collectives, grad_to_features(): lax.all_to_all(field, 'feat', split_axis=0, concat_axis=1, tiled=True)  66.3 us
    reduce_sum x16, other arithmetic, cluster_block(): jnp.sum(equality_mask.astype(jnp.float32), axis=0).astype(jnp.bfloat16)  57.2 us
  transfers between devices with their start and end apart: 9, of which 6 were waited for; matrix products, arithmetic and copies ran while one was open for 24% of the time, Pallas kernels for 0%

commit v1 on v0

v1 whole, which is shorter than its diff:
```python
import jax
import jax.numpy as jnp
from jax import lax
from jax.sharding import PartitionSpec as P


def activate(value):
    return jax.nn.gelu(value, approximate=True)


def body(features, neighbours, edge_counts, w_one, b_one, w_two, b_two, cotangent):
    nf = lax.axis_size("feat")
    capacity = edge_counts.shape[1]
    own = edge_counts.shape[0] // nf
    first = lax.axis_index("feat") * own
    near = lax.dynamic_slice_in_dim(neighbours, first, own, 0)
    totals = lax.dynamic_slice_in_dim(edge_counts, first, own, 0)
    steps = jnp.arange(near.shape[1], dtype=jnp.int32)
    near = jnp.where(steps[None, :, None] < totals[:, None, :], near, -1)
    slots = jnp.arange(capacity, dtype=jnp.int32)
    counts_t = jnp.sum(
        (near[:, :, None, :] == slots[None, None, :, None]).astype(jnp.float32), axis=1
    ).astype(jnp.bfloat16)
    live = totals.astype(jnp.float32)
    scaling = jnp.where(totals > 0, 1.0 / (live + 1.0), 0.0)

    w_one, w_two, b_one, b_two = (
        lax.all_gather(v, ("feat", "grp"), axis=0, tiled=True) for v in (w_one, w_two, b_one, b_two)
    )

    def aggregate(field):
        blocks = field.reshape(field.shape[0], own, capacity)
        summed = jnp.einsum("fuj,uji->fui", blocks, counts_t, preferred_element_type=jnp.float32)
        summed = summed + 2.0 * blocks.astype(jnp.float32)
        return (scaling[None] * summed).reshape(field.shape).astype(jnp.bfloat16)

    def aggregate_back(grad):
        blocks = grad.reshape(grad.shape[0], own, capacity).astype(jnp.float32)
        normed = (scaling[None] * blocks).astype(jnp.bfloat16)
        summed = jnp.einsum("fui,uji->fuj", normed, counts_t, preferred_element_type=jnp.float32)
        return (summed + 2.0 * normed.astype(jnp.float32)).reshape(grad.shape).astype(jnp.bfloat16)

    def linear(rows, weight, bias):
        product = lax.dot_general(
            weight, rows, (((0,), (0,)), ((), ())), preferred_element_type=jnp.float32
        )
        return product + bias.astype(jnp.float32)[:, None]

    def weight_term(rows, grad_pre):
        term = lax.dot_general(
            rows, grad_pre, (((1,), (1,)), ((), ())), preferred_element_type=jnp.float32
        )
        return lax.psum_scatter(
            term.astype(jnp.bfloat16), ("feat", "grp"), scatter_dimension=0, tiled=True
        ).astype(jnp.float32)

    def bias_term(grad_pre):
        return lax.psum_scatter(
            jnp.sum(grad_pre.astype(jnp.float32), axis=1),
            ("feat", "grp"),
            scatter_dimension=0,
            tiled=True,
        )

    field = lax.all_to_all(features, "feat", split_axis=1, concat_axis=0, tiled=True)
    rows_one = aggregate(field)
    pre_one = linear(rows_one, w_one, b_one)
    hidden, back_one = jax.vjp(activate, pre_one)
    rows_two = aggregate(hidden.astype(jnp.bfloat16))
    pre_two = linear(rows_two, w_two, b_two)
    output, back_two = jax.vjp(activate, pre_two)
    grad_pre_two = back_two(cotangent.astype(jnp.float32))[0].astype(jnp.bfloat16)
    grad_w_two = weight_term(rows_two, grad_pre_two)
    grad_rows_two = jnp.dot(w_two, grad_pre_two, preferred_element_type=jnp.float32)
    grad_hidden = aggregate_back(grad_rows_two.astype(jnp.bfloat16))
    grad_pre_one = back_one(grad_hidden.astype(jnp.float32))[0].astype(jnp.bfloat16)
    grad_w_one = weight_term(rows_one, grad_pre_one)
    grad_rows_one = jnp.dot(w_one, grad_pre_one, preferred_element_type=jnp.float32)
    grad_field = aggregate_back(grad_rows_one.astype(jnp.bfloat16))
    input_grad = lax.all_to_all(grad_field, "feat", split_axis=0, concat_axis=1, tiled=True)
    return (
        output.astype(jnp.bfloat16),
        input_grad.astype(jnp.float32),
        grad_w_one,
        bias_term(grad_pre_one),
        grad_w_two,
        bias_term(grad_pre_two),
    )


def solution(mesh):
    both = ("feat", "grp")
    in_specs = (
        P("feat", "grp"),
        P("grp", None, None),
        P("grp", None),
        P(both, None),
        P(both),
        P(both, None),
        P(both),
        P(None, ("grp", "feat")),
    )
    out_specs = (
        P(None, ("grp", "feat")),
        P("feat", "grp"),
        P(both, None),
        P(both),
        P(both, None),
        P(both),
    )
    return jax.shard_map(body, mesh=mesh, in_specs=in_specs, out_specs=out_specs, check_vma=False)
```

time: 1160 us -> 643 us (0.55)
  blocking collectives: 372 us -> 186 us
  waiting for transfers between devices: 378 us -> 237 us
  matrix products: 175 us -> 111 us
  local copies, waits for them, and re-layouts: 109 us -> 52.3 us
  other arithmetic: 77.3 us -> 22.7 us
  starting transfers between devices: 24 us -> 9.9 us
    all_to_all x4 -> x0, blocking collectives: 251 us -> none  [the longest x2 119 us: forward_pass(): lax.all_to_all(hidden_rows, 'feat', split_axis=0, concat_axis=1, tiled=True)]
    all_to_all x5 -> x2, waiting for transfers between devices: 204 us -> 0.01 us  [the longest x1 0.01 us: body(): lax.all_to_all(features, 'feat', split_axis=1, concat_axis=0, tiled=True)]
    unnamed x2, blocking collectives: 120 us -> 186 us
    reduce_scatter x2, waiting for transfers between devices: 151 us -> 216 us  [weight_term(): lax.psum_scatter(term.astype(jnp.bfloat16), ('feat', 'grp'), scatter_dime...]
    dot_general x14 -> x10, matrix products: 175 us -> 111 us  [the longest x2 37.1 us: linear(): lax.dot_general(weight, rows, (((0,), (0,)), ((), ())), preferred_element...]
    reduce_sum x17 -> x2, other arithmetic: 65.4 us -> 11.3 us  [the longest x1 6.96 us: bias_term(): jnp.sum(grad_pre.astype(jnp.float32), axis=1)]
    convert_element_type x5 -> x1, local copies, waits for them, and re-layouts: 27 us -> 2.85 us  [aggregate_back(): (summed + 2.0 * normed.astype(jnp.float32)).reshape(grad.shape)]
    all_to_all x5 -> x2, starting transfers between devices: 23.5 us -> 9.75 us  [the longest x1 5.17 us: body(): lax.all_to_all(features, 'feat', split_axis=1, concat_axis=0, tiled=True)]
  transfers between devices with their start and end apart: 9 -> 6, of which waited for: 6 -> 3; matrix products, arithmetic and copies ran while one was open for 24% -> 19% of each run, Pallas kernels for 0% -> 0%
where the time goes in v1:
time: 643 us; the launch traced here: 633 us
  waiting for transfers between devices  237 us (37%)
  blocking collectives  186 us (29%)
  matrix products  111 us (17%)
  local copies, waits for them, and re-layouts  52.3 us (8%)
  other arithmetic  22.7 us (4%)
  between operations  14.4 us (2%)
  starting transfers between devices  9.9 us (2%)
    reduce_scatter x2, waiting for transfers between devices, weight_term(): lax.psum_scatter(term.astype(jnp.bfloat16), ('feat', 'grp'), scatter_dime...  216 us
    unnamed x2, blocking collectives  186 us
    dot_general x2, matrix products, linear(): lax.dot_general(weight, rows, (((0,), (0,)), ((), ())), preferred_element...  37.1 us
    unnamed x27, local copies, waits for them, and re-layouts  35.4 us
    dot_general x2, matrix products, weight_term(): lax.dot_general(rows, grad_pre, (((1,), (1,)), ((), ())), preferred_eleme...  25.7 us
    all_gather x2, waiting for transfers between devices, body(): lax.all_gather(v, ('feat', 'grp'), axis=0, tiled=True)  19.4 us
    dot_general x2, matrix products, aggregate(): jnp.einsum('fuj,uji->fui', blocks, counts_t, preferred_element_type=jnp.f...  13.2 us
  transfers between devices with their start and end apart: 6, of which 3 were waited for; matrix products, arithmetic and copies ran while one was open for 19% of the time, Pallas kernels for 0%

profile of v1, /device:TPU:0, one launch (start us, length us, event | category | flops | bytes accessed | tf_op | source)
XLA Modules:
  0.0 633.0 jit_solution(9709162123503564572)
XLA Ops:
  7.2 0.0 all-gather.3.cloned.1.call-start
  7.2 0.7 all-gather.3.cloned.1.call-update
  7.9 0.0 all-gather.5.cloned.1.call-start
  7.9 0.7 all-gather.5.cloned.1.call-update
  8.7 6.4 %copy.54 = bf16[256,8192]{0,1:T(8,128)(2,1)} copy(bf16[256,8192]{1,0:T(8,128)(2,1)} %param.8) | data formatting | bytes 8388608 | tf_op args[0]
  15.0 5.2 all-to-all-start
  20.2 0.0 reduce-scatter.3.cloned.1.call-start
  20.3 0.2 dynamic-update-slice
  20.5 0.2 dynamic-update-slice.1
  20.8 93.8 %all-reduce.5 = (bf16[2048]{0:T(1024)(128)(2,1)S(1)}, bf16[2048]{0:T(1024)(128)(2,1)S(1)}) all-reduce(bf16[2048]{0:T(1024)(128)(2,1)S(1)} %dynamic-update-slice, bf16[2048]{0:T(1024)(128)(2,1)S(1)} %dynamic-update-slice.1), channel_id=1, replica_groups=mesh['feat'=8,'grp'=4] {'feat','grp'}, use_global_device_ids=true, to_apply=%add | all-reduce | flops 4096 | bytes 16384
  114.6 6.4 %copy.60 = bf16[2048,1024]{0,1:T(8,128)(2,1)} copy(bf16[2048,1024]{1,0:T(8,128)(2,1)} %param.15) | data formatting | bytes 8388608 | tf_op args[7]
  121.0 0.7 compare_select_fusion
  121.7 0.9 dynamic-slice_select_fusion
  122.6 4.4 convert_reduce_fusion
  127.0 6.6 %copy.55 = bf16[8,256,1024]{1,0,2:T(8,128)(2,1)} copy(bf16[8,256,1024]{1,2,0:T(8,128)(2,1)} %bitcast.1) | data formatting | bytes 8388608 | tf_op jit(solution)/shard_map/all_to_all | solution.py:65
  133.6 7.5 %reshape.49 = bf16[2048,2,512]{0,2,1:T(8,128)(2,1)} reshape(bf16[8,256,1024]{1,0,2:T(8,128)(2,1)} %copy.55) | data formatting | bytes 8388608 | tf_op jit(solution)/shard_map/reshape | solution.py:32
  141.1 8.2 %fusion.27 = bf16[2048,2,512]{0,2,1:T(8,128)(2,1)} fusion(bf16[2048,2,512]{0,2,1:T(8,128)(2,1)} %reshape.49, bf16[2,512,512]{2,1,0:T(8,128)(2,1)S(1)} %convert_reduce_fusion, f32[2,512]{1,0:T(2,128)S(1)} %get-tuple-element.44), kind=kOutput, calls=%fused_computation.43 | convolution fusion | flops 2157969408 | bytes 9441280 | tf_op jit(solution)/shard_map/fuj,uji->fui/dot_general | solution.py:33
  149.3 16.5 %fusion.25 = (bf16[2048,1024]{0,1:T(8,128)(2,1)S(1)}, f32[1024,2048]{1,0:T(8,128)}) fusion(f32[2048]{0:T(1024)S(1)} %convert_element_type.136, bf16[2048,1024]{0,1:T(8,128)(2,1)} %bitcast.101, bf16[2048,2048]{1,0:T(8,128)(2,1)} %all-gather.3.cloned.1.call-done), kind=kOutput, calls=%fused_computation.40 | convolution fusion | flops 8610906112 | bytes 25174016 | tf_op jit(solution)/shard_map/dot_general | solution.py:44
  165.8 5.0 fusion.24
  170.7 19.4 %all-gather.5.cloned.1.call-done = bf16[2048,2048]{1,0:T(8,128)(2,1)} async-done(((bf16[64,2048]{1,0:T(8,128)(2,1)}), bf16[2048,2048]{1,0:T(8,128)(2,1)}) %all-gather.5.cloned.1.call-update) | async-done | bytes 8388624 | tf_op jit(solution)/shard_map/all_gather | solution.py:28
  190.2 20.7 %convert_reduce_fusion.1 = (f32[2048]{0:T(1024)S(1)}, bf16[2048,1024]{0,1:T(8,128)(2,1)S(1)}, bf16[2048,1024]{0,1:T(8,128)(2,1)}) fusion(f32[2048]{0:T(1024)S(1)} %convert_element_type.141, bf16[2048,1024]{0,1:T(8,128)(2,1)} %copy.60, bf16[2048,1024]{0,1:T(8,128)(2,1)} %bitcast.99, bf16[2048,2048]{1,0:T(8,128)(2,1)} %all-gather.5.cloned.1.call-done), kind=kOutput, calls=%fused_computation.44 | convolution fusion | flops 8644458496 | bytes 25182208 | tf_op jit(solution)/shard_map/dot_general | solution.py:44
  210.8 2.1 copy-done.5
  212.9 11.2 %convert_convert_fusion.1 = f32[1024,2048]{1,0:T(8,128)} fusion(bf16[2048,1024]{0,1:T(8,128)(2,1)S(1)} %get-tuple-element.41, bf16[2048,2048]{1,0:T(8,128)(2,1)S(1)} %copy-done.1), kind=kOutput, calls=%fused_computation.51 | convolution fusion | flops 8594128896 | bytes 20971520 | tf_op jit(solution)/shard_map/dot_general | solution.py:74
  224.1 0.0 slice-start
  224.1 0.0 slice-start.1
  224.1 8.4 %fusion.21 = bf16[2048,2,512]{0,2,1:T(8,128)(2,1)S(1)} fusion(bf16[2,512,512]{2,1,0:T(8,128)(2,1)S(1)} %convert_reduce_fusion, f32[2048,2,512]{0,2,1:T(8,128)} %bitcast.98, f32[2,512]{1,0:T(2,128)S(1)} %get-tuple-element.44), kind=kOutput, calls=%fused_computation.33 | convolution fusion | flops 2164260864 | bytes 13635584 | tf_op jit(solution)/shard_map/fui,uji->fuj/dot_general | solution.py:40
  232.6 7.0 %convert_reduce_fusion.2 = (f32[2048]{0:T(1024)S(1)}, bf16[2048,1024]{0,1:T(8,128)(2,1)S(1)}) fusion(f32[1024,2048]{1,0:T(8,128)S(1)} %bitcast.95, f32[2048]{0:T(1024)S(1)} %convert_element_type.136, bf16[2048,2,512]{0,2,1:T(8,128)(2,1)S(1)} %fusion.21), kind=kLoop, calls=%fused_computation.45 | loop fusion | flops 50329600 | bytes 16793600 | tf_op jit(solution)/shard_map/reduce_sum | solution.py:59
  239.6 2.0 copy-done
  241.6 11.4 %convolution_convert_fusion.1 = bf16[2048,2048]{1,0:T(8,128)(2,1)} fusion(bf16[2048,1024]{0,1:T(8,128)(2,1)S(1)} %bitcast.102, bf16[2048,1024]{0,1:T(8,128)(2,1)S(1)} %get-tuple-element.43), kind=kOutput, calls=%fused_computation.49 | convolution fusion | flops 8594128896 | bytes 16777216 | tf_op jit(solution)/shard_map/dot_general | solution.py:50
  253.0 0.0 reduce-scatter.3.cloned.1.call-update
  253.0 0.0 reduce-scatter.5.cloned.1.call-start
  253.0 14.4 %convolution_convert_fusion = bf16[2048,2048]{1,0:T(8,128)(2,1)} fusion(bf16[2048,1024]{0,1:T(8,128)(2,1)} %bitcast.100, bf16[2048,1024]{0,1:T(8,128)(2,1)} %copy-done.5), kind=kOutput, calls=%fused_computation.48 | convolution fusion | flops 8594128896 | bytes 16777216 | tf_op jit(solution)/shard_map/dot_general | solution.py:50
  267.4 0.0 reduce-scatter.5.cloned.1.call-update
  267.4 12.6 %convert_convert_fusion = f32[1024,2048]{1,0:T(8,128)S(1)} fusion(bf16[2048,1024]{0,1:T(8,128)(2,1)} %copy-done, bf16[2048,2048]{1,0:T(8,128)(2,1)} %all-gather.3.cloned.1.call-done), kind=kOutput, calls=%fused_computation.50 | convolution fusion | flops 8594128896 | bytes 20971520 | tf_op jit(solution)/shard_map/dot_general | solution.py:78
  280.0 3.0 fusion.20
  283.0 1.5 copy.72
  284.5 2.9 copy.63
  287.4 4.6 all-to-all-start.1
  291.9 6.4 %copy.64 = bf16[2048,1024]{1,0:T(8,128)(2,1)} copy(bf16[2048,1024]{0,1:T(8,128)(2,1)} %get-tuple-element.46) | data formatting | bytes 8388608
  298.3 91.8 %all-reduce.4 = (f32[2048]{0:T(1024)S(1)}, f32[2048]{0:T(1024)S(1)}) all-reduce(f32[2048]{0:T(1024)S(1)} %get-tuple-element.42, f32[2048]{0:T(1024)S(1)} %get-tuple-element.40), channel_id=3, replica_groups=mesh['feat'=8,'grp'=4] {'feat','grp'}, use_global_device_ids=true, to_apply=%region_3.4.clone | all-reduce | flops 4096 | bytes 32768
  390.1 0.6 dynamic-slice
  390.7 0.6 dynamic-slice.1
  391.3 6.2 convert_element_type.178
  397.5 8.9 %copy.65 = f32[256,8192]{1,0:T(8,128)} copy(f32[256,8192]{0,1:T(8,128)} %bitcast.91) | data formatting | bytes 16777216
  406.4 32.2 %reduce-scatter.3.cloned.1.call-done = bf16[64,2048]{1,0:T(8,128)(2,1)} async-done(((bf16[2048,2048]{1,0:T(8,128)(2,1)}), bf16[64,2048]{1,0:T(8,128)(2,1)}) %reduce-scatter.3.cloned.1.call-update) | async-done | bytes 262160 | tf_op jit(solution)/shard_map/reduce_scatter | solution.py:53
  438.6 1.8 convert_element_type.167
  440.4 183.9 %reduce-scatter.5.cloned.1.call-done = bf16[64,2048]{1,0:T(8,128)(2,1)} async-done(((bf16[2048,2048]{1,0:T(8,128)(2,1)}), bf16[64,2048]{1,0:T(8,128)(2,1)}) %reduce-scatter.5.cloned.1.call-update) | async-done | bytes 262160 | tf_op jit(solution)/shard_map/reduce_scatter | solution.py:53
  624.3 1.8 convert_element_type.170
  (20 shorter events, 0.0 us)
Async XLA Ops:
  7.2 142.1 %all-gather.3.cloned.1.call-start = ((), (), s32[]{:S(2)}) async-start(), calls=%async_computation.4 | async-start | bytes 8650752 | tf_op jit(solution)/shard_map/all_gather | solution.py:28
  7.9 182.2 %all-gather.5.cloned.1.call-start = ((), (), s32[]{:S(2)}) async-start(), calls=%async_computation.5 | async-start | bytes 8650752 | tf_op jit(solution)/shard_map/all_gather | solution.py:28
  8.7 11.6 %copy-start.2 = (bf16[64]{0:T(256)(128)(2,1)S(1)}, bf16[64]{0:T(256)(128)(2,1)}, u32[]{:S(2)}) copy-start(bf16[64]{0:T(256)(128)(2,1)} %param.12) | copy-start | bytes 388
  8.7 11.9 %copy-start.3 = (bf16[64]{0:T(256)(128)(2,1)S(1)}, bf16[64]{0:T(256)(128)(2,1)}, u32[]{:S(2)}) copy-start(bf16[64]{0:T(256)(128)(2,1)} %param.14) | copy-start | bytes 388
  15.0 111.9 %all-to-all-start = ((bf16[256,8,1024]{0,2,1:T(8,128)(2,1)}), bf16[256,8,1024]{0,2,1:T(8,128)(2,1)}, u32[]{:S(2)}, u32[]{:S(2)}) async-start(bf16[256,8,1024]{0,2,1:T(8,128)(2,1)} %bitcast.92), calls=%async_computation | async-start | bytes 8388608 | tf_op jit(solution)/shard_map/all_to_all | solution.py:65
  20.2 418.4 %reduce-scatter.3.cloned.1.call-start = ((), (), s32[]{:S(2)}) async-start(), calls=%async_computation.6 | async-start | bytes 8650752 | tf_op jit(solution)/shard_map/reduce_scatter | solution.py:53
  190.2 22.7 %copy-start.1 = (bf16[2048,2048]{1,0:T(8,128)(2,1)S(1)}, bf16[2048,2048]{1,0:T(8,128)(2,1)}, u32[]{:S(2)}) copy-start(bf16[2048,2048]{1,0:T(8,128)(2,1)} %all-gather.5.cloned.1.call-done) | copy-start | bytes 25165828
  210.8 2.1 copy-start.5
  224.1 8.5 %slice-start = ((s8[8388608]{0:T(1024)(128)(4,1)}), s8[4194304]{0:T(1024)(128)(4,1)S(1)}, s32[]{:S(2)}) async-start(s8[8388608]{0:T(1024)(128)(4,1)} %bitcast.94), calls=%async_computation.8 | async-start | bytes 8388608
  224.1 8.5 %slice-start.1 = ((s8[8388608]{0:T(1024)(128)(4,1)}), s8[4194304]{0:T(1024)(128)(4,1)S(1)}, s32[]{:S(2)}) async-start(s8[8388608]{0:T(1024)(128)(4,1)} %bitcast.94), calls=%async_computation.9 | async-start | bytes 8388608
  232.6 9.0 %copy-start.4 = (bf16[2048,2,512]{0,2,1:T(8,128)(2,1)S(1)}, bf16[2048,2,512]{0,2,1:T(8,128)(2,1)}, u32[]{:S(2)}) copy-start(bf16[2048,2,512]{0,2,1:T(8,128)(2,1)} %fusion.27) | copy-start | bytes 12582916
  239.6 2.0 copy-start
  253.0 371.3 %reduce-scatter.5.cloned.1.call-start = ((), (), s32[]{:S(2)}) async-start(), calls=%async_computation.7 | async-start | bytes 8650752 | tf_op jit(solution)/shard_map/reduce_scatter | solution.py:53
  287.4 104.0 %all-to-all-start.1 = ((bf16[8,256,1024]{1,2,0:T(8,128)(2,1)}), bf16[8,256,1024]{1,2,0:T(8,128)(2,1)}, u32[]{:S(2)}, u32[]{:S(2)}) async-start(bf16[8,256,1024]{1,2,0:T(8,128)(2,1)} %copy.63), calls=%async_computation.1 | async-start | bytes 8388608 | tf_op jit(solution)/shard_map/all_to_all | solution.py:80
Sparse Core Ops, SparseCore 0:
  10.9 100.2 all-gather.2
  114.2 75.9 all-gather.4
  253.1 185.4 reduce-scatter.2
  440.8 183.4 reduce-scatter.4
